TPU v7x, 32 devices: a whole 2x2x4 slice. The times are simulated.
32 devices in a mesh: grid: 8 (over y, x, core), band: 4 (over z).
Axes of the slice: x: 2, y: 2, z: 4, core: 2. Of those that a mesh axis runs over, the one named last changes fastest.
Arguments:
- orbitals: float32 [256, 16, 8, 128], P('band', 'grid'), may hold values from -6 to 6
- potential: float32 [16, 8, 128], P('grid'), may hold values from -8 to 8
- rotation: float32 [256, 256], P(None, 'band'), may hold values from -0.375 to 0.375
Outputs:
- rotated: float32 [256, 16, 8, 128], P('band', 'grid')
All inputs are finite; a program needn't handle non-finite values.
Results may differ from a plain program's by a relative error of at most 0.00007.
Values sent between devices are 32-bit elements; how exact they have to be, the bound alone decides.
A program may use at most 64 MiB of HBM per device.

v0:
```python
import jax
import jax.numpy as jnp
from jax import lax
from jax.sharding import PartitionSpec as P

center_shift = 18.0
half_width = 16.0
spacing_square = 0.25


def padded_2(value, sides, width):
    for axis, dim in sides:
        devices, length = (lax.axis_size(axis), value.shape[dim])
        up = [(i, (i + 1) % devices) for i in range(devices)]
        down = [(j, i) for i, j in up]
        last = lax.slice_in_dim(value, length - width, length, axis=dim)
        leading = lax.slice_in_dim(value, 0, width, axis=dim)
        before = lax.ppermute(last, axis, up)
        after = lax.ppermute(leading, axis, down)
        value = jnp.concatenate([before, value, after], axis=dim)
    return value


def second_along(states, which_axis):
    nearer = jnp.roll(states, 1, which_axis) + jnp.roll(states, -1, which_axis)
    farther = jnp.roll(states, 2, which_axis) + jnp.roll(states, -2, which_axis)
    return (16.0 * nearer - farther - 30.0 * states) / (12.0 * spacing_square)


def scaled_apply(states, potential):
    padded = padded_2(states, (("grid", 1),), 2)
    thickness = states.shape[1]
    nearer = padded[:, 1 : thickness + 1] + padded[:, 3 : thickness + 3]
    farther = padded[:, 0:thickness] + padded[:, 4 : thickness + 4]
    along_x = (16.0 * nearer - farther - 30.0 * states) / (12.0 * spacing_square)
    laplace = along_x + second_along(states, 2) + second_along(states, 3)
    hamilton = -0.5 * laplace + potential[None] * states
    return (hamilton - center_shift * states) / half_width


def per_device(orbitals, potential, rotation):
    scaled_once = scaled_apply(orbitals, potential)
    filtered = 2.0 * scaled_apply(scaled_once, potential) - orbitals
    columns = lax.all_gather(rotation, "band", axis=1, tiled=True)
    mixed_rows = jnp.einsum(
        "ob,oxyz->bxyz",
        columns,
        lax.all_to_all(filtered, "band", split_axis=3, concat_axis=0, tiled=True),
        precision=lax.Precision.HIGHEST,
    )
    return lax.all_to_all(mixed_rows, "band", split_axis=0, concat_axis=3, tiled=True)


def solution(mesh):
    in_specs = (P("band", "grid", None, None), P("grid", None, None), P(None, "band"))
    out_specs = P("band", "grid", None, None)
    return jax.shard_map(
        per_device, mesh=mesh, in_specs=in_specs, out_specs=out_specs, check_vma=False
    )
```

profile of v0, /device:TPU:0, one launch (start us, length us, event | category | flops | bytes accessed | tf_op | source)
XLA Modules:
  0.0 92.8 jit_solution(17730144080614223811)
XLA Ops:
  0.0 0.0 copy-start
  0.0 0.5 collective-permute-start
  0.5 2.9 %collective-permute-start.1 = (f32[64,2,8,128]{3,2,1,0:T(8,128)}, f32[64,2,8,128]{3,2,1,0:T(8,128)S(1)}, u32[]{:S(2)}, u32[]{:S(2)}) collective-permute-start(f32[64,2,8,128]{3,2,1,0:T(8,128)} %param.3), channel_id=1, source_target_pairs={{4,0},{8,4},{12,8},{16,12},{20,16},{24,20},{28,24},{0,28},{5,1},{9... | collective-permute-start | bytes 1572872 | tf_op jit(solution)/shard_map/ppermute | solution.py:19
  3.4 1.3 %fusion.42 = (f32[64,2,7,128]{3,2,1,0:T(8,128)S(1)}, f32[64,2,7,128]{3,2,1,0:T(8,128)S(1)}) fusion(f32[64,2,8,128]{3,2,1,0:T(8,128)} %param.3), kind=kLoop, calls=%fused_computation.57 | loop fusion | bytes 1835008 | tf_op jit(solution)/shard_map/jit(_roll_static)/slice | solution.py:25
  4.7 0.0 copy-done
  4.7 0.1 fusion.44
  4.8 0.0 copy-start.2
  4.8 0.2 fusion.45
  5.0 0.2 fusion.46
  5.2 0.1 fusion.43
  5.3 0.1 fusion.41
  5.4 0.1 copy-done.2
  5.5 0.2 fusion.47
  5.7 0.2 fusion.48
  5.9 7.6 %collective-permute-done = f32[64,2,8,128]{3,2,1,0:T(8,128)S(1)} collective-permute-done((f32[64,2,8,128]{3,2,1,0:T(8,128)}, f32[64,2,8,128]{3,2,1,0:T(8,128)S(1)}, u32[]{:S(2)}, u32[]{:S(2)}) %collective-permute-start) | collective-permute-done | bytes 524320 | tf_op jit(solution)/shard_map/ppermute | solution.py:18
  13.5 1.5 %collective-permute-done.1 = f32[64,2,8,128]{3,2,1,0:T(8,128)S(1)} collective-permute-done((f32[64,2,8,128]{3,2,1,0:T(8,128)}, f32[64,2,8,128]{3,2,1,0:T(8,128)S(1)}, u32[]{:S(2)}, u32[]{:S(2)}) %collective-permute-start.1) | collective-permute-done | bytes 524320 | tf_op jit(solution)/shard_map/ppermute | solution.py:19
  15.0 1.1 %broadcast_multiply_fusion = (f32[64,2,8,128]{3,2,1,0:T(8,128)S(1)}, f32[64,2,8,128]{3,2,1,0:T(8,128)S(1)}) fusion(f32[64,2,8,128]{3,2,1,0:T(8,128)S(1)} %copy-done, f32[2,8,128]{2,1,0:T(8,128)S(1)} %copy-done.2, f32[64,2,8,2]{3,2,1,0:T(8,128)S(1)} %get-tuple-element.36, f32[64,2,8,126]{3,2,1,0:T(8,128)S(1)} %get-tuple-element.38, ...), kind=kLoop, calls=%fused_computation.46 | loop fusion | flops 4456448 | bytes 6823936 | tf_op jit(solution)/shard_map/div | solution.py:38
  16.1 0.2 fusion.34
  16.3 0.2 fusion.35
  16.5 0.2 fusion.36
  16.7 0.1 fusion.37
  16.8 0.1 fusion.38
  16.9 0.1 fusion.40
  17.0 1.7 %collective-permute-start.2 = (f32[64,2,8,128]{3,2,1,0:T(8,128)S(1)}, f32[64,2,8,128]{3,2,1,0:T(8,128)S(1)}, u32[]{:S(2)}, u32[]{:S(2)}) collective-permute-start(f32[64,2,8,128]{3,2,1,0:T(8,128)S(1)} %get-tuple-element.5), channel_id=1, source_target_pairs={{0,4},{4,8},{8,12},{12,16},{16,20},{20,24},{24,28},{28,0},{1,5},{5... | collective-permute-start | bytes 1572872 | tf_op jit(solution)/shard_map/ppermute | solution.py:18
  18.7 1.1 %collective-permute-start.3 = (f32[64,2,8,128]{3,2,1,0:T(8,128)S(1)}, f32[64,2,8,128]{3,2,1,0:T(8,128)S(1)}, u32[]{:S(2)}, u32[]{:S(2)}) collective-permute-start(f32[64,2,8,128]{3,2,1,0:T(8,128)S(1)} %get-tuple-element.5), channel_id=1, source_target_pairs={{4,0},{8,4},{12,8},{16,12},{20,16},{24,20},{28,24},{0,28},{5,1},{9... | collective-permute-start | bytes 1572872 | tf_op jit(solution)/shard_map/ppermute | solution.py:19
  19.8 0.1 fusion.39
  19.9 0.2 fusion.33
  20.1 11.3 %collective-permute-done.2 = f32[64,2,8,128]{3,2,1,0:T(8,128)S(1)} collective-permute-done((f32[64,2,8,128]{3,2,1,0:T(8,128)S(1)}, f32[64,2,8,128]{3,2,1,0:T(8,128)S(1)}, u32[]{:S(2)}, u32[]{:S(2)}) %collective-permute-start.2) | collective-permute-done | bytes 524320 | tf_op jit(solution)/shard_map/ppermute | solution.py:18
  31.4 0.0 collective-permute-done.3
  31.4 1.2 %fusion.10 = f32[64,2,8,128]{3,2,1,0:T(8,128)S(1)} fusion(f32[64,2,8,128]{3,2,1,0:T(8,128)S(1)} %copy-done, f32[64,2,8,128]{3,2,1,0:T(8,128)S(1)} %collective-permute-done.3, f32[64,2,8,128]{3,2,1,0:T(8,128)S(1)} %get-tuple-element.5, f32[64,2,8,128]{3,2,1,0:T(8,128)S(1)} %collective-permute-done.2, f32[64,2,7,128]{3,2,1,0:T(8,128)S(1)} %get-tuple-element.20, ...), kind=kLoop, calls=%fused_computation.12 | loop fusion | flops 4587520 | bytes 7348224 | tf_op jit(solution)/shard_map/sub | solution.py:43
  32.6 0.0 copy-start.1
  32.6 0.6 copy.33
  33.2 1.4 %reshape.2 = f32[4,1,32768]{2,1,0:T(1,128)} reshape(f32[128,2,8,64]{3,2,1,0:T(8,128)S(1)} %bitcast.21) | data formatting | bytes 1048576
  34.6 4.5 %all-to-all-start = ((f32[4,1,32768]{2,1,0:T(1,128)}), f32[4,1,32768]{2,1,0:T(1,128)S(1)}, u32[]{:S(2)}, u32[]{:S(2)}) async-start(f32[4,1,32768]{2,1,0:T(1,128)} %reshape.2), calls=%async_computation | async-start | bytes 1048576 | tf_op jit(solution)/shard_map/all_to_all | solution.py:48
  39.1 0.0 copy-done.1
  39.1 22.5 %all_gather.3 = f32[256,256]{0,1:T(8,128)S(1)} all-gather(f32[256,64]{0,1:T(8,128)S(1)} %copy-done.1), channel_id=1, replica_groups=mesh['grid'=8,'band'=4] {'band'}, dimensions={1}, use_global_device_ids=true | all-gather | bytes 327680 | tf_op jit(solution)/shard_map/all_gather | solution.py:44
  61.6 0.0 all-to-all-done
  61.6 0.5 broadcast.50
  62.2 2.1 %reduce = f32[4,32768]{1,0:T(4,128)S(1)} reduce(f32[4,1,32768]{2,1,0:T(1,128)S(1)} %all-to-all-done, f32[]{:T(128)} %broadcast.50), dimensions={1}, to_apply=%all_to_all.26.reduce_sub_computation | reduce | bytes 1048580 | tf_op jit(solution)/shard_map/all_to_all | solution.py:48
  64.3 0.5 reshape.3
  64.8 0.7 copy.35
  65.5 0.6 all_to_all.29
  66.1 0.6 convolution_bitcast_fusion
  66.8 1.3 %copy.36 = f32[256,2,8,32]{3,2,1,0:T(8,128)S(1)} copy(f32[256,2,8,32]{0,3,2,1:T(8,128)S(1)} %convolution_bitcast_fusion) | data formatting | bytes 1048576 | tf_op jit(solution)/shard_map/ob,oxyz->bxyz/dot_general | solution.py:45
  68.1 0.9 %reshape.4 = f32[4,1,32768]{2,1,0:T(1,128)S(1)} reshape(f32[256,2,8,32]{3,2,1,0:T(8,128)S(1)} %copy.36) | data formatting | bytes 1048576
  69.0 18.8 %all_to_all.36 = f32[4,1,32768]{2,1,0:T(1,128)S(1)} all-to-all(f32[4,1,32768]{2,1,0:T(1,128)S(1)} %reshape.4), channel_id=1, replica_groups=mesh['grid'=8,'band'=4] {'band'}, dimensions={0} | all-to-all | bytes 1048576 | tf_op jit(solution)/shard_map/all_to_all | solution.py:51
  87.8 2.1 %reduce.1 = f32[4,32768]{1,0:T(4,128)S(1)} reduce(f32[4,1,32768]{2,1,0:T(1,128)S(1)} %all_to_all.36, f32[]{:T(128)} %broadcast.50), dimensions={1}, to_apply=%all_to_all.30.reduce_sub_computation | reduce | bytes 1048580 | tf_op jit(solution)/shard_map/all_to_all | solution.py:51
  89.9 0.7 reshape.5
  90.6 1.1 %copy.37 = f32[4,64,2,8,32]{1,4,0,3,2:T(8,128)S(1)} copy(f32[4,64,2,8,32]{4,3,2,1,0:T(8,128)S(1)} %bitcast.19) | data formatting | bytes 1048576 | tf_op jit(solution)/shard_map/all_to_all | solution.py:51
  91.7 1.1 %copy.38 = f32[64,2,8,128]{3,2,1,0:T(8,128)} copy(f32[64,2,8,128]{0,3,2,1:T(8,128)S(1)} %bitcast.20) | data formatting | bytes 1048576 | tf_op jit(solution)/shard_map/all_to_all | solution.py:51
  (1 shorter events, 0.0 us)
Async XLA Ops:
  0.0 4.7 %copy-start = (f32[64,2,8,128]{3,2,1,0:T(8,128)S(1)}, f32[64,2,8,128]{3,2,1,0:T(8,128)}, u32[]{:S(2)}) copy-start(f32[64,2,8,128]{3,2,1,0:T(8,128)} %param.3) | copy-start | bytes 1572868
  0.0 13.5 %collective-permute-start = (f32[64,2,8,128]{3,2,1,0:T(8,128)}, f32[64,2,8,128]{3,2,1,0:T(8,128)S(1)}, u32[]{:S(2)}, u32[]{:S(2)}) collective-permute-start(f32[64,2,8,128]{3,2,1,0:T(8,128)} %param.3), channel_id=1, source_target_pairs={{0,4},{4,8},{8,12},{12,16},{16,20},{20,24},{24,28},{28,0},{1,5},{5... | collective-permute-start | bytes 1572872 | tf_op jit(solution)/shard_map/ppermute | solution.py:18
  0.5 14.5 %collective-permute-start.1 = (f32[64,2,8,128]{3,2,1,0:T(8,128)}, f32[64,2,8,128]{3,2,1,0:T(8,128)S(1)}, u32[]{:S(2)}, u32[]{:S(2)}) collective-permute-start(f32[64,2,8,128]{3,2,1,0:T(8,128)} %param.3), channel_id=1, source_target_pairs={{4,0},{8,4},{12,8},{16,12},{20,16},{24,20},{28,24},{0,28},{5,1},{9... | collective-permute-start | bytes 1572872 | tf_op jit(solution)/shard_map/ppermute | solution.py:19
  4.8 0.7 copy-start.2
  17.0 14.4 %collective-permute-start.2 = (f32[64,2,8,128]{3,2,1,0:T(8,128)S(1)}, f32[64,2,8,128]{3,2,1,0:T(8,128)S(1)}, u32[]{:S(2)}, u32[]{:S(2)}) collective-permute-start(f32[64,2,8,128]{3,2,1,0:T(8,128)S(1)} %get-tuple-element.5), channel_id=1, source_target_pairs={{0,4},{4,8},{8,12},{12,16},{16,20},{20,24},{24,28},{28,0},{1,5},{5... | collective-permute-start | bytes 1572872 | tf_op jit(solution)/shard_map/ppermute | solution.py:18
  18.7 12.7 %collective-permute-start.3 = (f32[64,2,8,128]{3,2,1,0:T(8,128)S(1)}, f32[64,2,8,128]{3,2,1,0:T(8,128)S(1)}, u32[]{:S(2)}, u32[]{:S(2)}) collective-permute-start(f32[64,2,8,128]{3,2,1,0:T(8,128)S(1)} %get-tuple-element.5), channel_id=1, source_target_pairs={{4,0},{8,4},{12,8},{16,12},{20,16},{24,20},{28,24},{0,28},{5,1},{9... | collective-permute-start | bytes 1572872 | tf_op jit(solution)/shard_map/ppermute | solution.py:19
  32.6 6.6 %copy-start.1 = (f32[256,64]{0,1:T(8,128)S(1)}, f32[256,64]{0,1:T(8,128)}, u32[]{:S(2)}) copy-start(f32[256,64]{0,1:T(8,128)} %param.5) | copy-start | bytes 196612
  34.6 27.0 %all-to-all-start = ((f32[4,1,32768]{2,1,0:T(1,128)}), f32[4,1,32768]{2,1,0:T(1,128)S(1)}, u32[]{:S(2)}, u32[]{:S(2)}) async-start(f32[4,1,32768]{2,1,0:T(1,128)} %reshape.2), calls=%async_computation | async-start | bytes 1048576 | tf_op jit(solution)/shard_map/all_to_all | solution.py:48
where the time goes:
time: 93.1 us; the launch traced here: 92.8 us
  blocking collectives  41.3 us (44%)
  waiting for transfers between devices  20.4 us (22%)
  local copies, waits for them, and re-layouts  13.1 us (14%)
  starting transfers between devices  10.7 us (11%)
  other arithmetic  6.57 us (7%)
    all_gather x1, blocking collectives, per_device(): columns = lax.all_gather(rotation, 'band', axis=1, tiled=True)  22.5 us
    ppermute x2, waiting for transfers between devices, padded_2(): before = lax.ppermute(last, axis, up)  18.9 us
    all_to_all x1, blocking collectives, per_device(): lax.all_to_all(mixed_rows, 'band', split_axis=0, concat_axis=3, tiled=True)  18.8 us
    all_to_all x1, starting transfers between devices, per_device(): lax.all_to_all(filtered, 'band', split_axis=3, concat_axis=0, tiled=True)  4.51 us
    ppermute x2, starting transfers between devices, padded_2(): after = lax.ppermute(leading, axis, down)  4.03 us
    unnamed x10, local copies, waits for them, and re-layouts  3.75 us
    slice x8, local copies, waits for them, and re-layouts, second_along(): nearer = jnp.roll(states, 1, which_axis) + jnp.roll(states, -1, which_axis)  2.38 us
    all_to_all x2, local copies, waits for them, and re-layouts, per_device(): lax.all_to_all(mixed_rows, 'band', split_axis=0, concat_axis=3, tiled=True)  2.2 us
  transfers between devices with their start and end apart: 5, of which 3 were waited for; matrix products, arithmetic and copies ran while one was open for 3% of the time, Pallas kernels for 0%

commit v1 on v0

--- a/solution.py
+++ b/solution.py
@@ -1,11 +1,16 @@
+import functools
+
 import jax
 import jax.numpy as jnp
 from jax import lax
+from jax.experimental import pallas as pl
+from jax.experimental.pallas import tpu as pltpu
 from jax.sharding import PartitionSpec as P
 
 center_shift = 18.0
 half_width = 16.0
 spacing_square = 0.25
+MESH = pl.DeviceIdType.MESH
 
 
 def padded_2(value, sides, width):
@@ -38,7 +43,7 @@
     return (hamilton - center_shift * states) / half_width
 
 
-def per_device(orbitals, potential, rotation):
+def by_halos(orbitals, potential, rotation):
     scaled_once = scaled_apply(orbitals, potential)
     filtered = 2.0 * scaled_apply(scaled_once, potential) - orbitals
     columns = lax.all_gather(rotation, "band", axis=1, tiled=True)
@@ -51,7 +56,230 @@
     return lax.all_to_all(mixed_rows, "band", split_axis=0, concat_axis=3, tiled=True)
 
 
+near_factor = -0.5 * 16.0 / (12.0 * spacing_square) / half_width
+far_factor = 0.5 / (12.0 * spacing_square) / half_width
+own_factor = 0.5 * 90.0 / (12.0 * spacing_square) / half_width
+
+
+def ring(value, by):
+    by = by % value.shape[0]
+    return jnp.concatenate([value[-by:], value[:-by]], axis=0)
+
+
+def apply_once(v, diagonal):
+    ny, nz = v.shape[1:]
+    near = ring(v, 1) + ring(v, -1)
+    far = ring(v, 2) + ring(v, -2)
+    near = near + pltpu.roll(v, 1, 1) + pltpu.roll(v, ny - 1, 1)
+    far = far + pltpu.roll(v, 2 % ny, 1) + pltpu.roll(v, (ny - 2) % ny, 1)
+    near = near + pltpu.roll(v, 1, 2) + pltpu.roll(v, nz - 1, 2)
+    far = far + pltpu.roll(v, 2, 2) + pltpu.roll(v, nz - 2, 2)
+    return near_factor * near + far_factor * far + diagonal * v
+
+
+def kernel(
+    grid, band,
+    orb_ref, pot_ref, rot_ref, out_ref,
+    states, potentials, rotations, filtered, cells, turned, final,
+    own_sem, orb_send, orb_recv, pot_send, pot_recv, rot_send, rot_recv,
+    cell_send, cell_recv, fin_send, fin_recv,
+):
+    g, z = lax.axis_index("grid"), lax.axis_index("band")
+    everyone = grid * band
+    me = z * grid + g
+    few = states.shape[0]
+    planes, ny, nz = orb_ref.shape[1:]
+    share = planes * ny // band
+    mine = orb_ref.shape[0]
+
+    barrier = pltpu.get_barrier_semaphore()
+
+    def greet(d, _):
+        to = lax.rem(me + d, everyone)
+        pl.semaphore_signal(
+            barrier, inc=1, device_id=(lax.rem(to, grid), to // grid), device_id_type=MESH
+        )
+        return _
+
+    lax.fori_loop(1, everyone, greet, 0)
+
+    own_orb = pltpu.make_async_copy(
+        orb_ref.at[pl.ds(g * few, few)],
+        states.at[:, pl.ds(g * planes, planes)],
+        own_sem,
+    )
+    own_orb.start()
+    potentials[pl.ds(g * planes, planes)] = pot_ref[...]
+    rotations[z] = rot_ref[...]
+    pl.semaphore_wait(barrier, everyone - 1)
+
+    def orb_copy(d):
+        to = lax.rem(g + d, grid)
+        return pltpu.make_async_remote_copy(
+            src_ref=orb_ref.at[pl.ds(to * few, few)],
+            dst_ref=states.at[:, pl.ds(g * planes, planes)],
+            send_sem=orb_send.at[d],
+            recv_sem=orb_recv.at[d],
+            device_id=(to, z),
+            device_id_type=MESH,
+        )
+
+    def pot_copy(d):
+        to = lax.rem(g + d, grid)
+        return pltpu.make_async_remote_copy(
+            src_ref=pot_ref,
+            dst_ref=potentials.at[pl.ds(g * planes, planes)],
+            send_sem=pot_send.at[d],
+            recv_sem=pot_recv.at[d],
+            device_id=(to, z),
+            device_id_type=MESH,
+        )
+
+    def rot_copy(d):
+        return pltpu.make_async_remote_copy(
+            src_ref=rot_ref,
+            dst_ref=rotations.at[z],
+            send_sem=rot_send.at[d],
+            recv_sem=rot_recv.at[d],
+            device_id=(g, lax.rem(z + d, band)),
+            device_id_type=MESH,
+        )
+
+    def cell_copy(d):
+        to = lax.rem(me + d, everyone)
+        row = (lax.rem(to, grid) * band + to // grid) * (share * few)
+        return pltpu.make_async_remote_copy(
+            src_ref=filtered.at[pl.ds(pl.multiple_of(row, 8), share * few)],
+            dst_ref=cells.at[me],
+            send_sem=cell_send.at[d],
+            recv_sem=cell_recv.at[d],
+            device_id=(lax.rem(to, grid), to // grid),
+            device_id_type=MESH,
+        )
+
+    def fin_copy(d):
+        to = lax.rem(z + d, band)
+        return pltpu.make_async_remote_copy(
+            src_ref=turned.at[to],
+            dst_ref=final.at[z],
+            send_sem=fin_send.at[d],
+            recv_sem=fin_recv.at[d],
+            device_id=(g, to),
+            device_id_type=MESH,
+        )
+
+    def start_all(copy, count):
+        def body(d, _):
+            copy(d).start()
+            return _
+
+        lax.fori_loop(1, count, body, 0)
+
+    def wait_all(copy, count):
+        def body(d, _):
+            copy(d).wait()
+            return _
+
+        lax.fori_loop(1, count, body, 0)
+
+    start_all(pot_copy, grid)
+    start_all(orb_copy, grid)
+    start_all(rot_copy, band)
+    own_orb.wait()
+    wait_all(pot_copy, grid)
+    wait_all(orb_copy, grid)
+
+    diagonal = (potentials[...] - center_shift) / half_width + own_factor
+
+    def filter_one(j, _):
+        v = states[j]
+        result = 2.0 * apply_once(apply_once(v, diagonal), diagonal) - v
+        rows = result.shape[0] * ny
+        filtered[pl.ds(j, rows, stride=few), :] = result.reshape(rows, nz)
+        return _
+
+    lax.fori_loop(0, few, filter_one, 0)
+
+    start_all(cell_copy, everyone)
+    row = (g * band + z) * (share * few)
+    cells[me] = filtered[pl.ds(pl.multiple_of(row, 8), share * few), :]
+    wait_all(rot_copy, band)
+    wait_all(cell_copy, everyone)
+
+    operand = jnp.concatenate(
+        [
+            cells[:, pl.ds(r * few, few), :].reshape(everyone * few, nz)
+            for r in range(share)
+        ],
+        axis=1,
+    )
+    for d in list(range(1, band)) + [0]:
+        to = lax.rem(z + d, band)
+        part = lax.dot_general(
+            rotations[to],
+            operand,
+            (((0,), (0,)), ((), ())),
+            precision=lax.Precision.HIGHEST,
+            preferred_element_type=jnp.float32,
+        )
+        for r in range(share):
+            piece = part[:, r * nz : (r + 1) * nz]
+            if d == 0:
+                out_ref[pl.ds(z * share + r, mine, stride=planes * ny), :] = piece
+            else:
+                turned[to, pl.ds(r * mine, mine), :] = piece
+        if d:
+            fin_copy(d).start()
+    for d in range(1, band):
+        fin_copy(d).wait()
+        of = lax.rem(z - d + band, band)
+        for r in range(share):
+            out_ref[pl.ds(of * share + r, mine, stride=planes * ny), :] = final[
+                of, pl.ds(r * mine, mine), :
+            ]
+
+
+def by_exchange(grid, band, orbitals, potential, rotation):
+    mine, planes, ny, nz = orbitals.shape
+    few, share = mine // grid, planes * ny // band
+    everyone = grid * band
+    f32, dma = jnp.float32, pltpu.SemaphoreType.DMA
+    vmem = pl.BlockSpec(memory_space=pltpu.VMEM)
+    rotated = pl.pallas_call(
+        functools.partial(kernel, grid, band),
+        out_shape=jax.ShapeDtypeStruct((mine * planes * ny, nz), f32),
+        in_specs=[pl.BlockSpec(memory_space=pl.ANY), vmem, vmem],
+        out_specs=vmem,
+        scratch_shapes=[
+            pltpu.VMEM((few, grid * planes, ny, nz), f32),
+            pltpu.VMEM((grid * planes, ny, nz), f32),
+            pltpu.VMEM((band,) + rotation.shape, f32),
+            pltpu.VMEM((grid * planes * ny * few, nz), f32),
+            pltpu.VMEM((everyone, share * few, nz), f32),
+            pltpu.VMEM((band, share * mine, nz), f32),
+            pltpu.VMEM((band, share * mine, nz), f32),
+            dma,
+            dma((grid,)), dma((grid,)), dma((grid,)), dma((grid,)),
+            dma((band,)), dma((band,)),
+            dma((everyone,)), dma((everyone,)),
+            dma((band,)), dma((band,)),
+        ],
+        compiler_params=pltpu.CompilerParams(
+            collective_id=0, has_side_effects=True, vmem_limit_bytes=32 * 1024 * 1024
+        ),
+    )(orbitals, potential, rotation)
+    return rotated.reshape(orbitals.shape)
+
+
 def solution(mesh):
+    grid, band = mesh.shape["grid"], mesh.shape["band"]
+
+    def per_device(orbitals, potential, rotation):
+        mine, planes, ny, _ = orbitals.shape
+        if mine % (8 * grid) == 0 and planes * ny % band == 0:
+            return by_exchange(grid, band, orbitals, potential, rotation)
+        return by_halos(orbitals, potential, rotation)
+
     in_specs = (P("band", "grid", None, None), P("grid", None, None), P(None, "band"))
     out_specs = P("band", "grid", None, None)
     return jax.shard_map(

time: 93.1 us -> 45.6 us (0.49)
  Pallas kernels: 0 us -> 42.6 us
  blocking collectives: 41.3 us -> 0 us
  waiting for transfers between devices: 20.4 us -> 0 us
  starting transfers between devices: 10.7 us -> 0 us
  local copies, waits for them, and re-layouts: 13.1 us -> 2.78 us
  other arithmetic: 6.57 us -> 0 us
    pallas_call x0 -> x1, Pallas kernels: none -> 42.6 us  [by_exchange(): pl.pallas_call(functools.partial(kernel, grid, band), out_shape=jax.Shape...]
    all_gather x1 -> x0, blocking collectives: 22.5 us -> none  [per_device(): columns = lax.all_gather(rotation, 'band', axis=1, tiled=True)]
    ppermute x4 -> x0, waiting for transfers between devices: 20.4 us -> none  [the longest x2 18.9 us: padded_2(): before = lax.ppermute(last, axis, up)]
    all_to_all x1 -> x0, blocking collectives: 18.8 us -> none  [per_device(): lax.all_to_all(mixed_rows, 'band', split_axis=0, concat_axis=3, tiled=True)]
    ppermute x4 -> x0, starting transfers between devices: 6.2 us -> none  [the longest x2 4.03 us: padded_2(): after = lax.ppermute(leading, axis, down)]
    all_to_all x1 -> x0, starting transfers between devices: 4.51 us -> none  [per_device(): lax.all_to_all(filtered, 'band', split_axis=3, concat_axis=0, tiled=True)]
    all_to_all x2 -> x0, other arithmetic: 4.28 us -> none  [the longest x1 2.14 us: per_device(): lax.all_to_all(mixed_rows, 'band', split_axis=0, concat_axis=3, tiled=True)]
    all_to_all x5 -> x0, local copies, waits for them, and re-layouts: 4.01 us -> none  [the longest x2 2.2 us: per_device(): lax.all_to_all(mixed_rows, 'band', split_axis=0, concat_axis=3, tiled=True)]
  transfers between devices with their start and end apart: 5 -> 0, of which waited for: 3 -> 0; matrix products, arithmetic and copies ran while one was open for 3% -> 0% of each run, Pallas kernels for 0% -> 0%
where the time goes in v1:
time: 45.6 us; the launch traced here: 45.4 us
  Pallas kernels  42.6 us (93%)
  local copies, waits for them, and re-layouts  2.78 us (6%)
    pallas_call x1, Pallas kernels, by_exchange(): pl.pallas_call(functools.partial(kernel, grid, band), out_shape=jax.Shape...  42.6 us
    unnamed x6, local copies, waits for them, and re-layouts  2.78 us

profile of v1, /device:TPU:0, one launch (start us, length us, event | category | flops | bytes accessed | tf_op | source)
XLA Modules:
  0.0 45.4 jit_solution(14899810437919240597)
XLA Ops:
  0.0 0.0 copy-start.1
  0.0 0.9 %copy.4.rot_ref = f32[256,64]{1,0:T(8,128)S(1)} copy(f32[256,64]{0,1:T(8,128)} %param.5) | data formatting | bytes 131072 | tf_op args[2]
  0.9 0.0 copy-done.1
  1.0 0.0 copy-start
  1.0 1.0 %copy-done = f32[64,2,8,128]{3,2,1,0:T(8,128)S(1)} copy-done((f32[64,2,8,128]{3,2,1,0:T(8,128)S(1)}, f32[64,2,8,128]{3,2,1,0:T(8,128)}, u32[]{:S(2)}) %copy-start) | copy-done | bytes 524312
  2.0 42.6 %shard_map.37 = f32[1024,128]{1,0:T(8,128)S(1)} custom-call(f32[64,2,8,128]{3,2,1,0:T(8,128)S(1)} %copy-done, f32[2,8,128]{2,1,0:T(8,128)S(1)} %copy-done.1, f32[256,64]{1,0:T(8,128)S(1)} %copy.4.rot_ref), custom_call_target="tpu_custom_call" | custom-call | tf_op jit(solution)/shard_map/pallas_call | solution.py:248
  44.6 0.8 %copy.6 = f32[64,2,8,128]{3,2,1,0:T(8,128)} copy(f32[64,2,8,128]{3,2,1,0:T(8,128)S(1)} %bitcast.1) | data formatting | bytes 1048576
Async XLA Ops:
  0.0 1.0 %copy-start.1 = (f32[2,8,128]{2,1,0:T(8,128)S(1)}, f32[2,8,128]{2,1,0:T(8,128)}, u32[]{:S(2)}) copy-start(f32[2,8,128]{2,1,0:T(8,128)} %pot_ref.1) | copy-start | bytes 24580
  1.0 1.0 %copy-start = (f32[64,2,8,128]{3,2,1,0:T(8,128)S(1)}, f32[64,2,8,128]{3,2,1,0:T(8,128)}, u32[]{:S(2)}) copy-start(f32[64,2,8,128]{3,2,1,0:T(8,128)} %orb_ref.1) | copy-start | bytes 1572868

commit v2 on v1

--- a/solution.py
+++ b/solution.py
@@ -77,17 +77,37 @@
     return near_factor * near + far_factor * far + diagonal * v
 
 
+def cell_rows(cells, share, part_of):
+    chunks, everyone, _, nz = cells.shape
+    if chunks == 1:
+        return [
+            cells[0, :, pl.ds(r * part_of, part_of), :].reshape(everyone * part_of, nz)
+            for r in range(share)
+        ]
+    rows = []
+    for pair in range(share // 2):
+        first = cells[0, :, pl.ds(pair * 8, 8), :]
+        second = cells[1, :, pl.ds(pair * 8, 8), :]
+        low = lax.broadcasted_iota(jnp.int32, first.shape, 1) < 4
+        even = jnp.where(low, first, pltpu.roll(second, 4, 1))
+        odd = jnp.where(low, pltpu.roll(first, 4, 1), second)
+        rows += [even.reshape(everyone * 8, nz), odd.reshape(everyone * 8, nz)]
+    return rows
+
+
 def kernel(
     grid, band,
     orb_ref, pot_ref, rot_ref, out_ref,
     states, potentials, rotations, filtered, cells, turned, final,
     own_sem, orb_send, orb_recv, pot_send, pot_recv, rot_send, rot_recv,
-    cell_send, cell_recv, fin_send, fin_recv,
+    spread_send, spread_recv, cell_send, cell_recv, fin_send, fin_recv,
 ):
     g, z = lax.axis_index("grid"), lax.axis_index("band")
     everyone = grid * band
     me = z * grid + g
     few = states.shape[0]
+    chunks = filtered.shape[0]
+    part_of = few // chunks
     planes, ny, nz = orb_ref.shape[1:]
     share = planes * ny // band
     mine = orb_ref.shape[0]
@@ -110,16 +130,16 @@
     )
     own_orb.start()
     potentials[pl.ds(g * planes, planes)] = pot_ref[...]
-    rotations[z] = rot_ref[...]
+    rotations[z, pl.ds(g * few, few)] = rot_ref[pl.ds(pl.multiple_of(g * few, 8), few)]
     pl.semaphore_wait(barrier, everyone - 1)
 
-    def orb_copy(d):
+    def orb_copy(c, d):
         to = lax.rem(g + d, grid)
         return pltpu.make_async_remote_copy(
-            src_ref=orb_ref.at[pl.ds(to * few, few)],
-            dst_ref=states.at[:, pl.ds(g * planes, planes)],
-            send_sem=orb_send.at[d],
-            recv_sem=orb_recv.at[d],
+            src_ref=orb_ref.at[pl.ds(to * few + c * part_of, part_of)],
+            dst_ref=states.at[pl.ds(c * part_of, part_of), pl.ds(g * planes, planes)],
+            send_sem=orb_send.at[c, d],
+            recv_sem=orb_recv.at[c, d],
             device_id=(to, z),
             device_id_type=MESH,
         )
@@ -137,22 +157,33 @@
 
     def rot_copy(d):
         return pltpu.make_async_remote_copy(
-            src_ref=rot_ref,
-            dst_ref=rotations.at[z],
+            src_ref=rot_ref.at[pl.ds(g * few, few)],
+            dst_ref=rotations.at[z, pl.ds(g * few, few)],
             send_sem=rot_send.at[d],
             recv_sem=rot_recv.at[d],
             device_id=(g, lax.rem(z + d, band)),
             device_id_type=MESH,
         )
 
-    def cell_copy(d):
+    def spread_copy(d):
+        rows = rotations.at[:, pl.ds(g * few, few)]
+        return pltpu.make_async_remote_copy(
+            src_ref=rows,
+            dst_ref=rows,
+            send_sem=spread_send.at[d],
+            recv_sem=spread_recv.at[d],
+            device_id=(lax.rem(g + d, grid), z),
+            device_id_type=MESH,
+        )
+
+    def cell_copy(c, d):
         to = lax.rem(me + d, everyone)
-        row = (lax.rem(to, grid) * band + to // grid) * (share * few)
-        return pltpu.make_async_remote_copy(
-            src_ref=filtered.at[pl.ds(pl.multiple_of(row, 8), share * few)],
-            dst_ref=cells.at[me],
-            send_sem=cell_send.at[d],
-            recv_sem=cell_recv.at[d],
+        row = (lax.rem(to, grid) * band + to // grid) * (share * part_of)
+        return pltpu.make_async_remote_copy(
+            src_ref=filtered.at[c, pl.ds(pl.multiple_of(row, 8), share * part_of)],
+            dst_ref=cells.at[c, me],
+            send_sem=cell_send.at[c, d],
+            recv_sem=cell_recv.at[c, d],
             device_id=(lax.rem(to, grid), to // grid),
             device_id_type=MESH,
         )
@@ -182,43 +213,41 @@
 
         lax.fori_loop(1, count, body, 0)
 
+    start_all(rot_copy, band)
     start_all(pot_copy, grid)
-    start_all(orb_copy, grid)
-    start_all(rot_copy, band)
+    for c in range(chunks):
+        start_all(functools.partial(orb_copy, c), grid)
     own_orb.wait()
     wait_all(pot_copy, grid)
-    wait_all(orb_copy, grid)
-
     diagonal = (potentials[...] - center_shift) / half_width + own_factor
-
-    def filter_one(j, _):
-        v = states[j]
-        result = 2.0 * apply_once(apply_once(v, diagonal), diagonal) - v
-        rows = result.shape[0] * ny
-        filtered[pl.ds(j, rows, stride=few), :] = result.reshape(rows, nz)
-        return _
-
-    lax.fori_loop(0, few, filter_one, 0)
-
-    start_all(cell_copy, everyone)
-    row = (g * band + z) * (share * few)
-    cells[me] = filtered[pl.ds(pl.multiple_of(row, 8), share * few), :]
+    own_row = pl.multiple_of((g * band + z) * (share * part_of), 8)
+    for c in range(chunks):
+        wait_all(functools.partial(orb_copy, c), grid)
+
+        def filter_one(j, _):
+            v = states[c * part_of + j]
+            result = 2.0 * apply_once(apply_once(v, diagonal), diagonal) - v
+            rows = result.shape[0] * ny
+            filtered[c, pl.ds(j, rows, stride=part_of), :] = result.reshape(rows, nz)
+            return _
+
+        lax.fori_loop(0, part_of, filter_one, 0)
+        start_all(functools.partial(cell_copy, c), everyone)
+        cells[c, me] = filtered[c, pl.ds(own_row, share * part_of), :]
+
     wait_all(rot_copy, band)
-    wait_all(cell_copy, everyone)
-
-    operand = jnp.concatenate(
-        [
-            cells[:, pl.ds(r * few, few), :].reshape(everyone * few, nz)
-            for r in range(share)
-        ],
-        axis=1,
-    )
+    start_all(spread_copy, grid)
+    wait_all(spread_copy, grid)
+    for c in range(chunks):
+        wait_all(functools.partial(cell_copy, c), everyone)
+
+    operand = jnp.concatenate(cell_rows(cells, share, part_of), axis=1)
     for d in list(range(1, band)) + [0]:
         to = lax.rem(z + d, band)
         part = lax.dot_general(
             rotations[to],
             operand,
-            (((0,), (0,)), ((), ())),
+            (((1,), (0,)), ((), ())),
             precision=lax.Precision.HIGHEST,
             preferred_element_type=jnp.float32,
         )
@@ -244,6 +273,7 @@
     few, share = mine // grid, planes * ny // band
     everyone = grid * band
     f32, dma = jnp.float32, pltpu.SemaphoreType.DMA
+    chunks = 2 if few == 8 and share % 2 == 0 else 1
     vmem = pl.BlockSpec(memory_space=pltpu.VMEM)
     rotated = pl.pallas_call(
         functools.partial(kernel, grid, band),
@@ -253,21 +283,21 @@
         scratch_shapes=[
             pltpu.VMEM((few, grid * planes, ny, nz), f32),
             pltpu.VMEM((grid * planes, ny, nz), f32),
-            pltpu.VMEM((band,) + rotation.shape, f32),
-            pltpu.VMEM((grid * planes * ny * few, nz), f32),
-            pltpu.VMEM((everyone, share * few, nz), f32),
+            pltpu.VMEM((band,) + rotation.shape[::-1], f32),
+            pltpu.VMEM((chunks, grid * planes * ny * few // chunks, nz), f32),
+            pltpu.VMEM((chunks, everyone, share * few // chunks, nz), f32),
             pltpu.VMEM((band, share * mine, nz), f32),
             pltpu.VMEM((band, share * mine, nz), f32),
             dma,
-            dma((grid,)), dma((grid,)), dma((grid,)), dma((grid,)),
-            dma((band,)), dma((band,)),
-            dma((everyone,)), dma((everyone,)),
+            dma((chunks, grid)), dma((chunks, grid)), dma((grid,)), dma((grid,)),
+            dma((band,)), dma((band,)), dma((grid,)), dma((grid,)),
+            dma((chunks, everyone)), dma((chunks, everyone)),
             dma((band,)), dma((band,)),
         ],
         compiler_params=pltpu.CompilerParams(
             collective_id=0, has_side_effects=True, vmem_limit_bytes=32 * 1024 * 1024
         ),
-    )(orbitals, potential, rotation)
+    )(orbitals, potential, rotation.T)
     return rotated.reshape(orbitals.shape)
 
 

time: 45.6 us -> 43.2 us (0.947)
  Pallas kernels: 42.6 us -> 39.4 us
  local copies, waits for them, and re-layouts: 2.78 us -> 3.37 us
    pallas_call x1, Pallas kernels: 42.6 us -> 39.4 us  [by_exchange(): pl.pallas_call(functools.partial(kernel, grid, band), out_shape=jax.Shape...]
    unnamed x6 -> x7, local copies, waits for them, and re-layouts: 2.78 us -> 3.37 us
where the time goes in v2:
time: 43.2 us; the launch traced here: 42.8 us
  Pallas kernels  39.4 us (91%)
  local copies, waits for them, and re-layouts  3.37 us (8%)
    pallas_call x1, Pallas kernels, by_exchange(): pl.pallas_call(functools.partial(kernel, grid, band), out_shape=jax.Shape...  39.4 us
    unnamed x7, local copies, waits for them, and re-layouts  3.37 us

profile of v2, /device:TPU:0, one launch (start us, length us, event | category | flops | bytes accessed | tf_op | source)
XLA Modules:
  0.0 42.8 jit_solution(1020172403818758229)
XLA Ops:
  0.0 0.0 copy-start
  0.0 1.0 %copy-done = f32[64,2,8,128]{3,2,1,0:T(8,128)S(1)} copy-done((f32[64,2,8,128]{3,2,1,0:T(8,128)S(1)}, f32[64,2,8,128]{3,2,1,0:T(8,128)}, u32[]{:S(2)}) %copy-start) | copy-done | bytes 524312
  1.0 0.0 copy-start.1
  1.0 0.8 %copy-done.1 = f32[256,64]{0,1:T(8,128)S(1)} copy-done((f32[256,64]{0,1:T(8,128)S(1)}, f32[256,64]{0,1:T(8,128)}, u32[]{:S(2)}) %copy-start.1) | copy-done | bytes 65560
  1.9 0.0 copy-start.2
  1.9 0.7 %copy-done.2 = f32[2,8,128]{2,1,0:T(8,128)S(1)} copy-done((f32[2,8,128]{2,1,0:T(8,128)S(1)}, f32[2,8,128]{2,1,0:T(8,128)}, u32[]{:S(2)}) %copy-start.2) | copy-done | bytes 8216
  2.6 39.4 %shard_map.37 = f32[1024,128]{1,0:T(8,128)S(1)} custom-call(f32[64,2,8,128]{3,2,1,0:T(8,128)S(1)} %copy-done, f32[2,8,128]{2,1,0:T(8,128)S(1)} %copy-done.2, f32[64,256]{1,0:T(8,128)S(1)} %bitcast.3), custom_call_target="tpu_custom_call" | custom-call | tf_op jit(solution)/shard_map/pallas_call | solution.py:278
  42.0 0.8 %copy.5 = f32[64,2,8,128]{3,2,1,0:T(8,128)} copy(f32[64,2,8,128]{3,2,1,0:T(8,128)S(1)} %bitcast.2) | data formatting | bytes 1048576
Async XLA Ops:
  0.0 1.0 %copy-start = (f32[64,2,8,128]{3,2,1,0:T(8,128)S(1)}, f32[64,2,8,128]{3,2,1,0:T(8,128)}, u32[]{:S(2)}) copy-start(f32[64,2,8,128]{3,2,1,0:T(8,128)} %orb_ref.1) | copy-start | bytes 1572868
  1.0 0.8 %copy-start.1 = (f32[256,64]{0,1:T(8,128)S(1)}, f32[256,64]{0,1:T(8,128)}, u32[]{:S(2)}) copy-start(f32[256,64]{0,1:T(8,128)} %param.5) | copy-start | bytes 196612
  1.9 0.7 %copy-start.2 = (f32[2,8,128]{2,1,0:T(8,128)S(1)}, f32[2,8,128]{2,1,0:T(8,128)}, u32[]{:S(2)}) copy-start(f32[2,8,128]{2,1,0:T(8,128)} %pot_ref.1) | copy-start | bytes 24580

commit v3 on v2

--- a/solution.py
+++ b/solution.py
@@ -95,6 +95,17 @@
     return rows
 
 
+def halves(value):
+    high = value.astype(jnp.bfloat16)
+    return high, (value - high.astype(jnp.float32)).astype(jnp.bfloat16)
+
+
+def dot(a, b):
+    return lax.dot_general(
+        a, b, (((1,), (0,)), ((), ())), preferred_element_type=jnp.float32
+    )
+
+
 def kernel(
     grid, band,
     orb_ref, pot_ref, rot_ref, out_ref,
@@ -200,18 +211,12 @@
         )
 
     def start_all(copy, count):
-        def body(d, _):
+        for d in range(1, count):
             copy(d).start()
-            return _
-
-        lax.fori_loop(1, count, body, 0)
 
     def wait_all(copy, count):
-        def body(d, _):
+        for d in range(1, count):
             copy(d).wait()
-            return _
-
-        lax.fori_loop(1, count, body, 0)
 
     start_all(rot_copy, band)
     start_all(pot_copy, grid)
@@ -241,15 +246,12 @@
     for c in range(chunks):
         wait_all(functools.partial(cell_copy, c), everyone)
 
-    operand = jnp.concatenate(cell_rows(cells, share, part_of), axis=1)
+    high, low = halves(jnp.concatenate(cell_rows(cells, share, part_of), axis=1))
     for d in list(range(1, band)) + [0]:
         to = lax.rem(z + d, band)
-        part = lax.dot_general(
-            rotations[to],
-            operand,
-            (((1,), (0,)), ((), ())),
-            precision=lax.Precision.HIGHEST,
-            preferred_element_type=jnp.float32,
+        turn_high, turn_low = halves(rotations[to])
+        part = (
+            dot(turn_low, high) + dot(turn_high, low) + dot(turn_high, high)
         )
         for r in range(share):
             piece = part[:, r * nz : (r + 1) * nz]

time: 43.2 us -> 42.9 us (level)
    pallas_call x1, Pallas kernels: 39.4 us -> 39 us  [by_exchange(): pl.pallas_call(functools.partial(kernel, grid, band), out_shape=jax.Shape...]
where the time goes in v3:
time: 42.9 us; the launch traced here: 42.4 us
  Pallas kernels  39 us (91%)
  local copies, waits for them, and re-layouts  3.37 us (8%)
    pallas_call x1, Pallas kernels, by_exchange(): pl.pallas_call(functools.partial(kernel, grid, band), out_shape=jax.Shape...  39 us
    unnamed x7, local copies, waits for them, and re-layouts  3.37 us

profile of v3, /device:TPU:0, one launch (start us, length us, event | category | flops | bytes accessed | tf_op | source)
XLA Modules:
  0.0 42.4 jit_solution(6662071825258403545)
XLA Ops:
  0.0 0.0 copy-start
  0.0 1.0 %copy-done = f32[64,2,8,128]{3,2,1,0:T(8,128)S(1)} copy-done((f32[64,2,8,128]{3,2,1,0:T(8,128)S(1)}, f32[64,2,8,128]{3,2,1,0:T(8,128)}, u32[]{:S(2)}) %copy-start) | copy-done | bytes 524312
  1.0 0.0 copy-start.1
  1.0 0.8 %copy-done.1 = f32[256,64]{0,1:T(8,128)S(1)} copy-done((f32[256,64]{0,1:T(8,128)S(1)}, f32[256,64]{0,1:T(8,128)}, u32[]{:S(2)}) %copy-start.1) | copy-done | bytes 65560
  1.9 0.0 copy-start.2
  1.9 0.7 %copy-done.2 = f32[2,8,128]{2,1,0:T(8,128)S(1)} copy-done((f32[2,8,128]{2,1,0:T(8,128)S(1)}, f32[2,8,128]{2,1,0:T(8,128)}, u32[]{:S(2)}) %copy-start.2) | copy-done | bytes 8216
  2.6 39.0 %shard_map.37 = f32[1024,128]{1,0:T(8,128)S(1)} custom-call(f32[64,2,8,128]{3,2,1,0:T(8,128)S(1)} %copy-done, f32[2,8,128]{2,1,0:T(8,128)S(1)} %copy-done.2, f32[64,256]{1,0:T(8,128)S(1)} %bitcast.3), custom_call_target="tpu_custom_call" | custom-call | tf_op jit(solution)/shard_map/pallas_call | solution.py:280
  41.6 0.8 %copy.5 = f32[64,2,8,128]{3,2,1,0:T(8,128)} copy(f32[64,2,8,128]{3,2,1,0:T(8,128)S(1)} %bitcast.2) | data formatting | bytes 1048576
Async XLA Ops:
  0.0 1.0 %copy-start = (f32[64,2,8,128]{3,2,1,0:T(8,128)S(1)}, f32[64,2,8,128]{3,2,1,0:T(8,128)}, u32[]{:S(2)}) copy-start(f32[64,2,8,128]{3,2,1,0:T(8,128)} %orb_ref.1) | copy-start | bytes 1572868
  1.0 0.8 %copy-start.1 = (f32[256,64]{0,1:T(8,128)S(1)}, f32[256,64]{0,1:T(8,128)}, u32[]{:S(2)}) copy-start(f32[256,64]{0,1:T(8,128)} %param.5) | copy-start | bytes 196612
  1.9 0.7 %copy-start.2 = (f32[2,8,128]{2,1,0:T(8,128)S(1)}, f32[2,8,128]{2,1,0:T(8,128)}, u32[]{:S(2)}) copy-start(f32[2,8,128]{2,1,0:T(8,128)} %pot_ref.1) | copy-start | bytes 24580

commit v4 on v3

--- a/solution.py
+++ b/solution.py
@@ -218,12 +218,13 @@
         for d in range(1, count):
             copy(d).wait()
 
+    start_all(pot_copy, grid)
+    start_all(functools.partial(orb_copy, 0), grid)
     start_all(rot_copy, band)
-    start_all(pot_copy, grid)
-    for c in range(chunks):
-        start_all(functools.partial(orb_copy, c), grid)
     own_orb.wait()
     wait_all(pot_copy, grid)
+    for c in range(1, chunks):
+        start_all(functools.partial(orb_copy, c), grid)
     diagonal = (potentials[...] - center_shift) / half_width + own_factor
     own_row = pl.multiple_of((g * band + z) * (share * part_of), 8)
     for c in range(chunks):

time: 42.9 us -> 42.6 us (level)
  the two profiles are of different devices: /device:TPU:0 before, /device:TPU:24 now
where the time goes in v4:
time: 42.6 us; the launch traced here: 42.3 us
  Pallas kernels  38.9 us (91%)
  local copies, waits for them, and re-layouts  3.37 us (8%)
    pallas_call x1, Pallas kernels, by_exchange(): pl.pallas_call(functools.partial(kernel, grid, band), out_shape=jax.Shape...  38.9 us
    unnamed x7, local copies, waits for them, and re-layouts  3.37 us

profile of v4, /device:TPU:24, one launch (start us, length us, event | category | flops | bytes accessed | tf_op | source)
XLA Modules:
  0.0 42.3 jit_solution(10820290677533330658)
XLA Ops:
  0.0 0.0 copy-start
  0.0 1.0 %copy-done = f32[64,2,8,128]{3,2,1,0:T(8,128)S(1)} copy-done((f32[64,2,8,128]{3,2,1,0:T(8,128)S(1)}, f32[64,2,8,128]{3,2,1,0:T(8,128)}, u32[]{:S(2)}) %copy-start) | copy-done | bytes 524312
  1.0 0.0 copy-start.1
  1.0 0.8 %copy-done.1 = f32[256,64]{0,1:T(8,128)S(1)} copy-done((f32[256,64]{0,1:T(8,128)S(1)}, f32[256,64]{0,1:T(8,128)}, u32[]{:S(2)}) %copy-start.1) | copy-done | bytes 65560
  1.9 0.0 copy-start.2
  1.9 0.7 %copy-done.2 = f32[2,8,128]{2,1,0:T(8,128)S(1)} copy-done((f32[2,8,128]{2,1,0:T(8,128)S(1)}, f32[2,8,128]{2,1,0:T(8,128)}, u32[]{:S(2)}) %copy-start.2) | copy-done | bytes 8216
  2.6 38.9 %shard_map.37 = f32[1024,128]{1,0:T(8,128)S(1)} custom-call(f32[64,2,8,128]{3,2,1,0:T(8,128)S(1)} %copy-done, f32[2,8,128]{2,1,0:T(8,128)S(1)} %copy-done.2, f32[64,256]{1,0:T(8,128)S(1)} %bitcast.3), custom_call_target="tpu_custom_call" | custom-call | tf_op jit(solution)/shard_map/pallas_call | solution.py:281
  41.5 0.8 %copy.5 = f32[64,2,8,128]{3,2,1,0:T(8,128)} copy(f32[64,2,8,128]{3,2,1,0:T(8,128)S(1)} %bitcast.2) | data formatting | bytes 1048576
Async XLA Ops:
  0.0 1.0 %copy-start = (f32[64,2,8,128]{3,2,1,0:T(8,128)S(1)}, f32[64,2,8,128]{3,2,1,0:T(8,128)}, u32[]{:S(2)}) copy-start(f32[64,2,8,128]{3,2,1,0:T(8,128)} %orb_ref.1) | copy-start | bytes 1572868
  1.0 0.8 %copy-start.1 = (f32[256,64]{0,1:T(8,128)S(1)}, f32[256,64]{0,1:T(8,128)}, u32[]{:S(2)}) copy-start(f32[256,64]{0,1:T(8,128)} %param.5) | copy-start | bytes 196612
  1.9 0.7 %copy-start.2 = (f32[2,8,128]{2,1,0:T(8,128)S(1)}, f32[2,8,128]{2,1,0:T(8,128)}, u32[]{:S(2)}) copy-start(f32[2,8,128]{2,1,0:T(8,128)} %pot_ref.1) | copy-start | bytes 24580
